TPU v7x, 512 devices: a whole 4x8x8 slice. The times are simulated.
512 devices in a mesh: rows: 256 (over x, z, y), cols: 2 (over core).
Axes of the slice: x: 4, y: 8, z: 8, core: 2. Of those that a mesh axis runs over, the one named last changes fastest.
Arguments:
- row_points: float32 [3, 131072], P(None, 'rows')
- panel_points: bfloat16 [3, 8192], P(None, ('rows', 'cols')), may hold values from 0 to 1
- test_vectors: bfloat16 [128, 8192], P(None, ('rows', 'cols')), may hold values from -0.0625 to 0.0625
- leaf_skeleton: int32 [256, 64], P('rows'), may hold values from 0 to 511, as said below
- node_skeleton: int32 [256, 4, 64], P('rows'), may hold values from 0 to 127, as said below
Outputs:
- leaf_interp: float32 [64, 131072], P(None, ('rows', 'cols'))
- transfers: float32 [256, 4, 64, 128], P('rows')
- top_skeleton: float32 [256, 64, 256], P('rows')
Inputs may be any that keep to these rules, and one draw needn't show every extreme that they name: `leaf_skeleton`: each leaf's 64 entries are distinct. `node_skeleton`: each entry list holds 64 distinct positions among the 128 stacked rows (the lower child's first); all leaves under the same node have the same list at that level.
All inputs are finite; a program needn't handle non-finite values.
Results may differ from a plain program's by a relative error of at most 0.0049.
Values may be sent and summed in bfloat16 or wider, within the bound.
A program may use at most 64 MiB of HBM per device.

v0:
```python
import math

import jax
import jax.numpy as jnp
from jax import lax
from jax.sharding import PartitionSpec as P

KAPPA = 40.0
SMOOTH = 0.05
RIDGE = 0.1
EPSILON = 1e-05


def from_partner(shard, axis, bit):
    return lax.ppermute(shard, axis, [(i, i ^ 1 << bit) for i in range(lax.axis_size(axis))])


def kernel_block(targets, sources):
    source_f = sources.astype(jnp.float32)
    dist_sq = jnp.zeros((targets.shape[1], source_f.shape[1]), jnp.float32)
    for component in range(3):
        offset = targets[component][:, None] - source_f[component][None, :]
        dist_sq = dist_sq + offset * offset
    radius = jnp.sqrt(dist_sq + SMOOTH * SMOOTH)
    real_part = (jnp.cos(KAPPA * radius) / radius).astype(jnp.bfloat16)
    imag_part = (jnp.sin(KAPPA * radius) / radius).astype(jnp.bfloat16)
    return (real_part, imag_part)


def sample_block(real_part, imag_part, vectors):
    first_half = jnp.dot(real_part, vectors.T, preferred_element_type=jnp.float32)
    second_half = jnp.dot(imag_part, vectors.T, preferred_element_type=jnp.float32)
    return jnp.concatenate([first_half, second_half], axis=1)


def interpolate(block, skeleton):
    gram_matrix = jnp.dot(skeleton, skeleton.T, precision=lax.Precision.HIGHEST)
    ridge = RIDGE * skeleton.shape[1] * (jnp.mean(skeleton * skeleton) + EPSILON)
    gram_matrix = gram_matrix + ridge * jnp.eye(skeleton.shape[0], dtype=jnp.float32)
    factor = jnp.linalg.cholesky(gram_matrix)
    right_side = jnp.dot(skeleton, block.T, precision=lax.Precision.HIGHEST)
    middle = lax.linalg.triangular_solve(factor, right_side, left_side=True, lower=True)
    return lax.linalg.triangular_solve(factor, middle, left_side=True, lower=True, transpose_a=True)


def body(row_points, panel_points, test_vectors, leaf_skeleton, node_skeleton):
    rows_here = row_points.shape[1]
    vec_count = test_vectors.shape[0]
    level_count = node_skeleton.shape[1]
    zero_sum = jnp.zeros((rows_here, 2 * vec_count), jnp.float32)
    running = zero_sum
    vectors = lax.all_gather(test_vectors, "rows", axis=1, tiled=True)
    sources = lax.all_gather(panel_points, "rows", axis=1, tiled=True)
    piece_width = vectors.shape[1]
    block_width = math.gcd(piece_width, 512)
    block_count = piece_width // block_width
    vec_blocks = jnp.moveaxis(vectors.reshape(vec_count, block_count, block_width), 1, 0)
    src_blocks = jnp.moveaxis(sources.reshape(3, block_count, block_width), 1, 0)

    def one_block(acc_sum, blocks):
        real_part, imag_part = kernel_block(row_points, blocks[1])
        return (acc_sum + sample_block(real_part, imag_part, blocks[0]), None)

    running, unused = lax.scan(one_block, running, (vec_blocks, src_blocks))
    half_rows = rows_here // lax.axis_size("cols")
    col_index = lax.axis_index("cols")
    samples = lax.psum(running, "cols")
    skel_rows = jnp.take(samples, leaf_skeleton[0], axis=0)
    own_samples = lax.dynamic_slice_in_dim(samples, col_index * half_rows, half_rows, 0)
    leaf_interp = interpolate(own_samples, skel_rows)
    row_index = lax.axis_index("rows")
    current = skel_rows
    level_maps = []
    for tree_level in range(level_count):
        partner = from_partner(current, "rows", tree_level)
        is_upper = jnp.right_shift(row_index, tree_level) & 1 == 1
        lower_child = jnp.where(is_upper, partner, current)
        upper_child = jnp.where(is_upper, current, partner)
        stacked = jnp.concatenate([lower_child, upper_child], axis=0)
        current = jnp.take(stacked, node_skeleton[0, tree_level], axis=0)
        level_maps.append(interpolate(stacked, current))
    path_maps = jnp.stack(level_maps)
    return (leaf_interp, path_maps[None], current[None])


def solution(mesh):
    placed = (
        P(None, "rows"),
        P(None, ("rows", "cols")),
        P(None, ("rows", "cols")),
        P("rows", None),
        P("rows", None, None),
    )
    return jax.shard_map(
        body,
        mesh=mesh,
        in_specs=placed,
        out_specs=(P(None, ("rows", "cols")), P("rows", None, None, None), P("rows", None, None)),
        check_vma=False,
    )
```

profile of v0, /device:TPU:1, one launch (start us, length us, event | category | flops | bytes accessed | tf_op | source)
XLA Modules:
  0.0 915.9 jit_solution(5012811315206166909)
XLA Ops:
  8.6 579.6 %all-gather = bf16[256,16,3]{1,2,0:T(4,128)(2,1)S(1)} all-gather(bf16[1,16,3]{1,2,0:T(4,128)(2,1)S(1)} %bitcast.174), channel_id=1, replica_groups=mesh['rows'=256,'cols'=2] {'rows'}, dimensions={0}, use_global_device_ids=true | all-gather | bytes 24672 | tf_op jit(solution)/shard_map/all_gather | solution.py:53
  590.6 88.6 %while.11 = (s32[]{:T(128)}, f32[512,256]{0,1:T(8,128)S(1)}, f32[3,512]{1,0:T(4,128)S(1)}, bf16[8,3,512]{2,1,0:T(4,128)(2,1)S(1)}, bf16[8,128,512]{1,2,0:T(8,128)(2,1)}, /*index=5*/s32[]{:T(128)}, s32[]{:T(128)}) while((s32[]{:T(128)}, f32[512,256]{0,1:T(8,128)S(1)}, f32[3,512]{1,0:T(4,128)S(1)}, bf16[8,3,512]{2,1,0:T(4,128)(2,1)S(1)}, ...), condition=%wide.region_1.2_spmd.clone, body=%wide.region_0.1_spmd.clone.sunk | while | flops 140903936 | bytes 2418779 | solution.py:64
  590.6 5.4 fusion.110
  596.0 5.4 fusion.109
  601.7 5.4 fusion.110
  607.1 5.4 fusion.109
  612.8 5.4 fusion.110
  618.2 5.4 fusion.109
  623.8 5.4 fusion.110
  629.2 5.4 fusion.109
  634.9 5.4 fusion.110
  640.3 5.4 fusion.109
  646.0 5.4 fusion.110
  651.4 5.4 fusion.109
  657.1 5.4 fusion.110
  662.5 5.4 fusion.109
  668.1 5.4 fusion.110
  673.5 5.4 fusion.109
  680.3 135.4 %all-reduce.2.cloned.1.call-done = f32[512,256]{1,0:T(8,128)} async-done(((f32[512,256]{1,0:T(8,128)}), f32[512,256]{1,0:T(8,128)}) %all-reduce.2.cloned.1.call-update) | async-done | bytes 524304 | tf_op jit(solution)/shard_map/psum | solution.py:67
  821.4 5.8 cholesky.89
  828.8 4.9 custom-call.13
  836.9 4.0 collective-permute-start.1
  841.9 5.8 cholesky.100
  849.0 4.9 custom-call.22
  856.0 4.4 collective-permute-start.2
  861.4 5.8 cholesky.111
  868.6 4.9 custom-call.24
  875.5 3.5 collective-permute-start.3
  880.0 5.8 cholesky.122
  887.2 4.9 custom-call.26
  895.9 5.8 cholesky.133
  903.0 4.9 custom-call.28
  (132 shorter events, 30.5 us)
Async XLA Ops:
  7.2 582.8 %all-gather.3.cloned.1.call-start = ((), (), s32[]{:S(2)}) async-start(), calls=%async_computation | async-start | bytes 1052672 | tf_op jit(solution)/shard_map/all_gather | solution.py:52
  7.9 807.8 %all-reduce.2.cloned.1.call-start = ((), (), s32[]{:S(2)}) async-start(), calls=%async_computation.1 | async-start | bytes 1048576 | tf_op jit(solution)/shard_map/psum | solution.py:67
  8.0 0.7 copy-start.3
  588.5 0.7 copy-start.4
  589.2 0.7 copy-start.2
  589.9 0.7 copy-start.1
  815.7 18.1 %copy-start = (f32[512,256]{1,0:T(8,128)S(1)}, f32[512,256]{1,0:T(8,128)}, u32[]{:S(2)}) copy-start(f32[512,256]{1,0:T(8,128)} %all-reduce.2.cloned.1.call-done) | copy-start | bytes 1572868
  818.1 17.1 %collective-permute-start = (f32[64,256]{1,0:T(8,128)S(1)}, f32[64,256]{1,0:T(8,128)S(1)}, u32[]{:S(2)}, u32[]{:S(2)}) collective-permute-start(f32[64,256]{1,0:T(8,128)S(1)} %get-tuple-element.88), channel_id=1, source_target_pairs={{0,2},{2,0},{4,6},{6,4},{8,10},{10,8},{12,14},{14,12},{16,18},{18,... | collective-permute-start | bytes 196616 | tf_op jit(solution)/shard_map/ppermute | solution.py:15
  836.9 17.5 %collective-permute-start.1 = (f32[64,256]{1,0:T(8,128)S(1)}, f32[64,256]{1,0:T(8,128)S(1)}, u32[]{:S(2)}, u32[]{:S(2)}) collective-permute-start(f32[64,256]{1,0:T(8,128)S(1)} %get-tuple-element.74), channel_id=1, source_target_pairs={{0,4},{2,6},{4,0},{6,2},{8,12},{10,14},{12,8},{14,10},{16,20},{18,... | collective-permute-start | bytes 196616 | tf_op jit(solution)/shard_map/ppermute | solution.py:15
  856.0 17.9 %collective-permute-start.2 = (f32[64,256]{1,0:T(8,128)S(1)}, f32[64,256]{1,0:T(8,128)S(1)}, u32[]{:S(2)}, u32[]{:S(2)}) collective-permute-start(f32[64,256]{1,0:T(8,128)S(1)} %get-tuple-element.76), channel_id=1, source_target_pairs={{0,8},{2,10},{4,12},{6,14},{8,0},{10,2},{12,4},{14,6},{16,24},{18,... | collective-permute-start | bytes 196616 | tf_op jit(solution)/shard_map/ppermute | solution.py:15
  875.5 17.0 %collective-permute-start.3 = (f32[64,256]{1,0:T(8,128)S(1)}, f32[64,256]{1,0:T(8,128)S(1)}, u32[]{:S(2)}, u32[]{:S(2)}) collective-permute-start(f32[64,256]{1,0:T(8,128)S(1)} %get-tuple-element.78), channel_id=1, source_target_pairs={{0,16},{2,18},{4,20},{6,22},{8,24},{10,26},{12,28},{14,30},{16,0},... | collective-permute-start | bytes 196616 | tf_op jit(solution)/shard_map/ppermute | solution.py:15
Sparse Core Ops, SparseCore 0:
  12.1 114.6 all-gather.2
  680.3 135.2 all-reduce.1
where the time goes:
time: 917 us; the launch traced here: 916 us
  blocking collectives  580 us (63%)
  waiting for transfers between devices  136 us (15%)
  matrix products  91.8 us (10%)
  other arithmetic  66.9 us (7%)
  between operations  17.8 us (2%)
  starting transfers between devices  14.3 us (2%)
    all_gather x1, blocking collectives, body(): sources = lax.all_gather(panel_points, 'rows', axis=1, tiled=True)  580 us
    psum x1, waiting for transfers between devices, body(): samples = lax.psum(running, 'cols')  135 us
    dot_general x8, matrix products, sample_block(): jnp.dot(imag_part, vectors.T, preferred_element_type=jnp.float32)  43.4 us
    dot_general x8, matrix products, sample_block(): jnp.dot(real_part, vectors.T, preferred_element_type=jnp.float32)  43.1 us
    another operation x15, other arithmetic, interpolate(): factor = jnp.linalg.cholesky(gram_matrix)  32.7 us
    another operation x10, other arithmetic, interpolate(): lax.linalg.triangular_solve(factor, middle, left_side=True, lower=True, t...  27.8 us
  transfers between devices with their start and end apart: 6, of which 1 were waited for; matrix products, arithmetic and copies ran while one was open for 6% of the time, Pallas kernels for 0%

commit v1 on v0

v1 whole, which is shorter than its diff:
```python
import functools
import math

import jax
import jax.numpy as jnp
from jax import lax
from jax.experimental import pallas as pl
from jax.experimental.pallas import tpu as pltpu
from jax.sharding import PartitionSpec as P

KAPPA = 40.0
SMOOTH = 0.05
RIDGE = 0.1
EPSILON = 1e-05

MESH = pl.DeviceIdType.MESH
HI = lax.Precision.HIGHEST
NT = (((1,), (1,)), ((), ()))
F32 = jnp.float32
BF16 = jnp.bfloat16

NX, NZ, NY = 4, 8, 8
LEAF = 512
VEC = 128
SK = 64
LEVELS = 4
TREE = LEVELS * SK
ROWS = LEAF + TREE
HALF = LEAF // 2
POOL = HALF + SK + TREE
UNIT = 256
GROUPS = ((0, 8),)

TURNS = KAPPA / (2.0 * math.pi)
SIN_C = (4.442867902958649, -7.307443418384947, 3.5947880506885697, -0.7843739567847821)
COS_C = (1.41421349656788, -6.97885098835421, 5.739461171797141, -1.8835629903414894, 0.3106981920345144)


def horner(q, coefs):
    out = q * coefs[-1] + coefs[-2]
    for c in coefs[-3::-1]:
        out = out * q + c
    return out


def kernel_values(dist_sq):
    inv = lax.rsqrt(dist_sq)
    turns = (dist_sq * inv) * TURNS
    frac = turns - jnp.round(turns)
    q = frac * frac
    sin_half = horner(q, SIN_C) * frac
    cos_half = horner(q, COS_C)
    scaled = inv * sin_half
    return (inv - scaled * sin_half).astype(BF16), (scaled * cos_half).astype(BF16)


def split3(v):
    hi = v.astype(BF16).astype(F32)
    mid = (v - hi).astype(BF16).astype(F32)
    lo = (v - hi - mid).astype(BF16).astype(F32)
    return hi, mid, lo


def stack_rows(rows, width):
    idx = lax.broadcasted_iota(jnp.int32, (16, width), 0)
    out = jnp.zeros((16, width), F32)
    for i, r in enumerate(rows):
        out = jnp.where(idx == i, jnp.broadcast_to(r, (16, width)), out)
    return out


def source_features(points):
    y = [points[i : i + 1, :] for i in range(3)]
    norm = split3(y[0] * y[0] + y[1] * y[1] + y[2] * y[2])
    one = jnp.ones_like(y[0])
    return stack_rows(y * 3 + list(norm) + [one] * 3, points.shape[1])


def target_features(points):
    x = [points[i : i + 1, :] for i in range(3)]
    parts = [split3(-2.0 * v) for v in x]
    norm = split3(x[0] * x[0] + x[1] * x[1] + x[2] * x[2] + SMOOTH * SMOOTH)
    one = jnp.ones_like(x[0])
    rows = [parts[k][s] for s in range(3) for k in range(3)]
    return stack_rows(rows + [one] * 3 + list(norm), points.shape[1])


def target_rows(points):
    feats = target_features(points)
    return jnp.concatenate([feats] * 8, axis=0).T.astype(BF16)


def pick_points(points, picks):
    n = points.shape[1]
    hot = lax.broadcasted_iota(jnp.int32, (n, SK), 0) == picks
    return jnp.dot(points, hot.astype(F32), precision=HI, preferred_element_type=F32)


def group_rows(g):
    return (GROUPS[g][1] + 1) * 16


def group_base(g):
    return sum(32 * group_rows(i) for i in range(g))


def ring_dist(t, n):
    return min(t % n, -t % n)


LINE = (4, 3, 5, 2, 6, 1, 7)
PLANE = sorted(
    [(i, k) for i in range(NX) for k in range(NZ) if (i, k) != (0, 0)],
    key=lambda t: ring_dist(t[0], NX) + ring_dist(t[1], NZ),
)


def sample_kernel(
    pts_ref, panel_ref, vec_ref, lskel_ref, nskel_ref, lskel_s, out_ref,
    raw, gath, tgt, u_s, k_re, k_im, acc, own_s, swap_tx, swap_rx, rx,
    raw_send, raw_recv, g_send, g_recv, t_send, t_recv, x_send, x_recv,
):
    row = lax.axis_index("rows")
    col = lax.axis_index("cols")
    x, z, y = row // 64, (row // 8) % 8, row % 8
    first = col == 0
    a = jnp.where(first, y, z)
    b = jnp.where(first, z, y)
    step_a = jnp.where(first, 1, 8)
    step_b = jnp.where(first, 8, 1)

    def on_line(j):
        return {"rows": row + ((a + j) % 8 - a) * step_a}

    def on_plane(i, k):
        return {"rows": row + ((x + i) % 4 - x) * 64 + ((b + k) % 8 - b) * step_b}

    barrier = pltpu.get_barrier_semaphore()
    peers = [on_line(j) for j in LINE] + [on_plane(*t) for t in PLANE] + [{"cols": 1 - col}]
    for peer in peers:
        pl.semaphore_signal(barrier, inc=1, device_id=peer, device_id_type=MESH)

    eye = (
        lax.broadcasted_iota(jnp.int32, (16, 16), 0) == lax.broadcasted_iota(jnp.int32, (16, 16), 1)
    ).astype(BF16)
    mine = pl.ds(pl.multiple_of(a * 32, 32), 16)
    mine_f = pl.ds(pl.multiple_of(a * 32 + 16, 16), 16)
    mine_both = pl.ds(pl.multiple_of(a * 32, 32), 32)
    raw[mine] = lax.dot_general(eye, vec_ref[...], NT, preferred_element_type=F32).astype(BF16)
    feats = jnp.concatenate([source_features(panel_ref[...].astype(F32))] * 8, axis=0)
    slot = lax.broadcasted_iota(jnp.int32, (128, 16), 0) // 16
    feats = jnp.where(slot == a, feats, 0.0).astype(BF16)
    raw[mine_f] = lax.dot_general(eye, feats, NT, preferred_element_type=F32).astype(BF16)

    pl.semaphore_wait(barrier, len(peers))

    for j in LINE:
        pltpu.make_async_remote_copy(
            raw.at[mine_both], raw.at[mine_both], raw_send, raw_recv.at[j], device_id=on_line(j), device_id_type=MESH
        ).start()

    zero_row = jnp.zeros((5, LEAF), F32)
    points = jnp.concatenate([pts_ref[...], zero_row], axis=0)
    current = pick_points(points, lskel_ref[...])

    def swap_copy(lev):
        bit = (row // (1 << lev)) % 2
        return pltpu.make_async_remote_copy(
            swap_tx.at[lev], swap_rx.at[lev], t_send.at[lev], t_recv.at[lev],
            device_id={"rows": row + (1 - 2 * bit) * (1 << lev)}, device_id_type=MESH,
        )

    def swap_start(lev, cur):
        bit = (row // (1 << lev)) % 2
        wide = jnp.concatenate([cur, cur], axis=1)
        upper = lax.broadcasted_iota(jnp.int32, (8, 2 * SK), 1) // SK
        swap_tx[lev] = jnp.where(upper == bit, wide, 0.0)
        swap_copy(lev).start()

    def swap_finish(lev):
        swap_copy(lev).wait_recv()
        bit = (row // (1 << lev)) % 2
        got = swap_rx[lev]
        other = jnp.where(bit == 1, got[:, :SK], got[:, SK:])
        tgt[LEAF + lev * SK : LEAF + (lev + 1) * SK] = target_rows(other)
        both = swap_tx[lev] + got
        return pick_points(both, nskel_ref[lev : lev + 1, :])

    swap_start(0, current)
    tgt[0:LEAF] = target_rows(pts_ref[...])
    acc[...] = jnp.zeros_like(acc)

    def block_copy(g, n, i, k):
        rows = group_rows(g)
        base = group_base(g)
        return pltpu.make_async_remote_copy(
            gath.at[pl.ds(base, rows)], gath.at[pl.ds(base + n * rows, rows)], g_send.at[g], g_recv.at[g, n],
            device_id=on_plane(i, k), device_id_type=MESH,
        )

    def send_group(g):
        start, count = GROUPS[g]
        base = group_base(g)
        for j in range(1, 8):
            src = (a + 8 - j) % 8
            needed = jnp.logical_and(src >= start, src < start + count)

            @pl.when(needed)
            def _():
                pltpu.make_async_remote_copy(
                    raw.at[mine_both], raw.at[mine_both], raw_send, raw_recv.at[j], device_id=on_line(j), device_id_type=MESH
                ).wait_recv()

        feat = jnp.zeros((16, 128), BF16)
        for i in range(count):
            at = (start + i) * 32
            gath[base + 16 * i : base + 16 * i + 16] = raw[at : at + 16]
            feat = feat + raw[at + 16 : at + 32]
        gath[base + 16 * count : base + 16 * count + 16] = feat
        for n, (i, k) in enumerate(PLANE):
            block_copy(g, n + 1, i, k).start()

    lane = lax.broadcasted_iota(jnp.int32, (16, 128), 1) // 16

    def compute_unit(g, unit):
        start, count = GROUPS[g]
        rows = group_rows(g)
        srcs = UNIT // (16 * count)
        vecs, feats = [], []
        for s in range(srcs):
            n = unit * srcs + s

            @pl.when(n > 0)
            def _():
                block_copy(g, n, 0, 1).wait_recv()

            at = group_base(g) + n * rows
            vecs.append(gath[pl.ds(pl.multiple_of(at, 16), 16 * count)])
            tile = gath[pl.ds(pl.multiple_of(at + 16 * count, 16), 16)]
            for j in range(start, start + count):
                feats.append(jnp.where(lane == j, tile, jnp.zeros_like(tile)))
        feat = jnp.concatenate(feats, axis=0)
        vec = jnp.concatenate(vecs, axis=0)
        u_s[...] = lax.dot_general(tgt[...], feat, NT, preferred_element_type=F32)
        for r in range(0, ROWS, 32):
            re, im = kernel_values(u_s[r : r + 32])
            k_re[r : r + 32] = re
            k_im[r : r + 32] = im
        acc[:, :VEC] += jnp.dot(k_re[...], vec, preferred_element_type=F32)
        acc[:, VEC:] += jnp.dot(k_im[...], vec, preferred_element_type=F32)

    for g in range(len(GROUPS)):
        send_group(g)
    for lev in range(LEVELS):
        current = swap_finish(lev)
        if lev + 1 < LEVELS:
            swap_start(lev + 1, current)
    for g in range(len(GROUPS)):
        units = 32 * 16 * GROUPS[g][1] // UNIT

        def step(u, carry, g=g):
            compute_unit(g, u)
            return carry

        lax.fori_loop(0, units, step, 0)

    for k in range(SK):
        own_s[k : k + 1] = acc[pl.ds(lskel_s[0, k], 1)]
    theirs = pl.ds(pl.multiple_of((1 - col) * HALF, HALF), HALF)
    ours = pl.ds(pl.multiple_of(col * HALF, HALF), HALF)
    spans = (
        (acc.at[theirs], rx.at[pl.ds(0, HALF)]),
        (own_s, rx.at[pl.ds(HALF, SK)]),
        (acc.at[pl.ds(LEAF, TREE)], rx.at[pl.ds(HALF + SK, TREE)]),
    )
    copies = [
        pltpu.make_async_remote_copy(
            src, dst, x_send.at[i], x_recv.at[i], device_id={"cols": 1 - col}, device_id_type=MESH
        )
        for i, (src, dst) in enumerate(spans)
    ]
    for c in copies:
        c.start()
    for c in copies:
        c.wait_recv()
    out_ref[0:HALF] = acc[ours] + rx[0:HALF]
    out_ref[HALF : HALF + SK] = own_s[...] + rx[HALF : HALF + SK]
    out_ref[HALF + SK : POOL] = acc[LEAF:ROWS] + rx[HALF + SK : POOL]

    for c in copies:
        c.wait_send()
    for lev in range(LEVELS):
        swap_copy(lev).wait_send()
    for j in LINE:
        pltpu.make_async_remote_copy(
            raw.at[mine_both], raw.at[mine_both], raw_send, raw_recv.at[j], device_id=on_line(j), device_id_type=MESH
        ).wait_send()
    for g in range(len(GROUPS)):
        for n, (i, k) in enumerate(PLANE):
            block_copy(g, n + 1, i, k).wait_send()


def sample_rows(row_points, panel_points, test_vectors, leaf_skeleton, node_skeleton):
    vmem = pl.BlockSpec(memory_space=pltpu.VMEM)
    n_groups = len(GROUPS)
    gath_rows = group_base(n_groups)
    dma = pltpu.SemaphoreType.DMA
    return pl.pallas_call(
        sample_kernel,
        out_shape=jax.ShapeDtypeStruct((POOL, 2 * VEC), F32),
        in_specs=[vmem] * 5 + [pl.BlockSpec(memory_space=pltpu.SMEM)],
        out_specs=vmem,
        scratch_shapes=[
            pltpu.VMEM((256, 128), BF16),
            pltpu.VMEM((gath_rows, 128), BF16),
            pltpu.VMEM((ROWS, 128), BF16),
            pltpu.VMEM((ROWS, UNIT), F32),
            pltpu.VMEM((ROWS, UNIT), BF16),
            pltpu.VMEM((ROWS, UNIT), BF16),
            pltpu.VMEM((ROWS, 2 * VEC), F32),
            pltpu.VMEM((SK, 2 * VEC), F32),
            pltpu.VMEM((LEVELS, 8, 2 * SK), F32),
            pltpu.VMEM((LEVELS, 8, 2 * SK), F32),
            pltpu.VMEM((POOL, 2 * VEC), F32),
            dma,
            dma((8,)),
            dma((n_groups,)),
            dma((n_groups, 32)),
            dma((LEVELS,)),
            dma((LEVELS,)),
            dma((3,)),
            dma((3,)),
        ],
        compiler_params=pltpu.CompilerParams(collective_id=1, has_side_effects=True, vmem_limit_bytes=40 << 20),
        name="sample_rows",
    )(row_points, panel_points, test_vectors, leaf_skeleton, node_skeleton[0], leaf_skeleton)


SPREAD = 1.0 + SK / RIDGE
NEWTON = 7


def solve_kernel(pool_ref, nskel_s, interp_ref, maps_ref, top_ref, stacks, skels):
    row = lax.axis_index("rows")
    for lev in range(LEVELS):
        bit = (row // (1 << lev)) % 2
        lower = pl.ds(pl.multiple_of(bit * SK, SK), SK)
        upper = pl.ds(pl.multiple_of((1 - bit) * SK, SK), SK)
        own = pool_ref[HALF : HALF + SK] if lev == 0 else skels[lev - 1]
        stacks[lev, lower] = own
        stacks[lev, upper] = pool_ref[HALF + (lev + 1) * SK : HALF + (lev + 2) * SK]
        for k in range(SK):
            skels[lev, k : k + 1] = stacks[lev, pl.ds(nskel_s[lev, k], 1)]
    top_ref[0] = skels[LEVELS - 1]

    systems = [(pool_ref[HALF : HALF + SK], pool_ref[0:HALF])]
    systems += [(skels[lev], stacks[lev]) for lev in range(LEVELS)]
    eye = (
        lax.broadcasted_iota(jnp.int32, (SK, SK), 0) == lax.broadcasted_iota(jnp.int32, (SK, SK), 1)
    ).astype(F32)

    def mm(p, q):
        return jnp.dot(p, q, precision=HI, preferred_element_type=F32)

    work = []
    for skel, block in systems:
        gram = lax.dot_general(skel, skel, NT, precision=HI, preferred_element_type=F32)
        right = lax.dot_general(skel, block, NT, precision=HI, preferred_element_type=F32)
        mean = jnp.sum(skel * skel) / (SK * 2 * VEC)
        lam = RIDGE * 2 * VEC * (mean + EPSILON)
        scale = 2.0 / ((SPREAD + 1.0) * lam)
        work.append((gram * scale + (2.0 / (SPREAD + 1.0)) * eye, right * scale))
    err = (SPREAD - 1.0) / (SPREAD + 1.0)
    inverses = [eye] * len(work)
    prods = [m for m, _ in work]
    for it in range(NEWTON):
        factor = 2.0 / (2.0 - err * err)
        err = err * err / (2.0 - err * err)
        next_inv, next_prod = [], []
        for inv, prod in zip(inverses, prods):
            left = (2.0 * eye - prod) * factor
            next_inv.append(left if it == 0 else mm(left, inv))
            next_prod.append(mm(left, prod) if it + 1 < NEWTON else prod)
        inverses, prods = next_inv, next_prod
    sols = [mm(inv, right) for inv, (_, right) in zip(inverses, work)]
    rest = [right - mm(m, sol) for sol, (m, right) in zip(sols, work)]
    sols = [sol + mm(inv, r) for sol, inv, r in zip(sols, inverses, rest)]
    interp_ref[...] = sols[0]
    for lev in range(LEVELS):
        maps_ref[0, lev] = sols[lev + 1]


def solve(pool, node_skeleton):
    vmem = pl.BlockSpec(memory_space=pltpu.VMEM)
    return pl.pallas_call(
        solve_kernel,
        out_shape=(
            jax.ShapeDtypeStruct((SK, HALF), F32),
            jax.ShapeDtypeStruct((1, LEVELS, SK, 2 * SK), F32),
            jax.ShapeDtypeStruct((1, SK, 2 * VEC), F32),
        ),
        in_specs=[vmem, pl.BlockSpec(memory_space=pltpu.SMEM)],
        out_specs=(vmem, vmem, vmem),
        scratch_shapes=[pltpu.VMEM((LEVELS, 2 * SK, 2 * VEC), F32), pltpu.VMEM((LEVELS, SK, 2 * VEC), F32)],
        compiler_params=pltpu.CompilerParams(vmem_limit_bytes=40 << 20),
        name="solve",
    )(pool, node_skeleton[0])


def body(row_points, panel_points, test_vectors, leaf_skeleton, node_skeleton):
    pool = sample_rows(row_points, panel_points, test_vectors, leaf_skeleton, node_skeleton)
    return solve(pool, node_skeleton)


def solution(mesh):
    placed = (
        P(None, "rows"),
        P(None, ("rows", "cols")),
        P(None, ("rows", "cols")),
        P("rows", None),
        P("rows", None, None),
    )
    return jax.shard_map(
        body,
        mesh=mesh,
        in_specs=placed,
        out_specs=(P(None, ("rows", "cols")), P("rows", None, None, None), P("rows", None, None)),
        check_vma=False,
    )
```

time: 917 us -> 64.5 us (0.07)
  blocking collectives: 580 us -> 0 us
  waiting for transfers between devices: 136 us -> 0 us
  matrix products: 91.8 us -> 0 us
  other arithmetic: 66.9 us -> 0 us
  Pallas kernels: 0 us -> 62.4 us
  between operations: 17.8 us -> 0.7 us
  starting transfers between devices: 14.3 us -> 0 us
    all_gather x1 -> x0, blocking collectives: 580 us -> none  [body(): sources = lax.all_gather(panel_points, 'rows', axis=1, tiled=True)]
    psum x1 -> x0, waiting for transfers between devices: 135 us -> none  [body(): samples = lax.psum(running, 'cols')]
    dot_general x26 -> x0, matrix products: 89 us -> none  [the longest x8 43.4 us: sample_block(): jnp.dot(imag_part, vectors.T, preferred_element_type=jnp.float32)]
    pallas_call x0 -> x2, Pallas kernels: none -> 62.4 us  [the longest x1 57.7 us: sample_rows(): pl.pallas_call(sample_kernel, out_shape=jax.ShapeDtypeStruct((POOL, 2 * V...]
    another operation x25 -> x0, other arithmetic: 60.4 us -> none  [the longest x15 32.7 us: interpolate(): factor = jnp.linalg.cholesky(gram_matrix)]
    ppermute x4 -> x0, starting transfers between devices: 14.2 us -> none  [from_partner(): lax.ppermute(shard, axis, [(i, i ^ 1 << bit) for i in range(lax.axis_size...]
  transfers between devices with their start and end apart: 6 -> 0, of which waited for: 1 -> 0; matrix products, arithmetic and copies ran while one was open for 6% -> 0% of each run, Pallas kernels for 0% -> 0%
where the time goes in v1:
time: 64.5 us; the launch traced here: 63.9 us
  Pallas kernels  62.4 us (97%)
  local copies, waits for them, and re-layouts  0.84 us (1%)
  between operations  0.7 us (1%)
    pallas_call x1, Pallas kernels, sample_rows(): pl.pallas_call(sample_kernel, out_shape=jax.ShapeDtypeStruct((POOL, 2 * V...  57.7 us
    pallas_call x1, Pallas kernels, solve(): pl.pallas_call(solve_kernel, out_shape=(jax.ShapeDtypeStruct((SK, HALF),...  4.73 us

profile of v1, /device:TPU:1, one launch (start us, length us, event | category | flops | bytes accessed | tf_op | source)
XLA Modules:
  0.0 63.9 jit_solution(6962123560346575225)
XLA Ops:
  0.6 0.0 copy-start
  0.6 0.0 copy-start.1
  0.7 0.0 copy-start.2
  0.7 0.0 copy-start.3
  0.7 0.8 %copy.8.vec_ref = bf16[128,16]{1,0:T(8,128)(2,1)S(1)} copy(bf16[128,16]{0,1:T(8,128)(2,1)} %param.7) | data formatting | bytes 8192 | tf_op args[2]
  1.5 0.0 copy-done
  1.5 0.0 copy-done.1
  1.5 0.0 copy-done.2
  1.5 0.0 copy-done.3
  1.5 57.7 %sample_rows.1.pool_ref = f32[576,256]{1,0:T(8,128)S(1)} custom-call(f32[3,512]{1,0:T(4,128)S(1)} %copy-done, bf16[3,16]{1,0:T(4,128)(2,1)S(1)} %copy-done.3, bf16[128,16]{1,0:T(8,128)(2,1)S(1)} %copy.8.vec_ref, s32[1,64]{1,0:T(1,128)S(1)} %copy-done.2, s32[4,64]{1,0:T(4,128)S(1)} %bitcast.1, s32[1,64]{1,0:T(1,128)S(1)} %copy-done.2), custom_call_target="tpu_custom_call" | custom-call | tf_op jit(solution)/shard_map/sample_rows/pallas_call | solution.py:308
  59.2 4.7 %solve.1 = (f32[64,256]{1,0:T(8,128)}, f32[1,4,64,128]{3,2,1,0:T(8,128)}, f32[1,64,256]{2,1,0:T(8,128)}) custom-call(f32[576,256]{1,0:T(8,128)S(1)} %sample_rows.1.pool_ref, s32[4,64]{1,0:T(4,128)S(1)} %bitcast.2), custom_call_target="tpu_custom_call" | custom-call | tf_op jit(solution)/shard_map/solve/pallas_call | solution.py:395
Async XLA Ops:
  0.6 0.9 %copy-start = (f32[3,512]{1,0:T(4,128)S(1)}, f32[3,512]{1,0:T(4,128)}, u32[]{:S(2)}) copy-start(f32[3,512]{1,0:T(4,128)} %pts_ref.1) | copy-start | bytes 18436
  0.6 0.9 %copy-start.1 = (s32[1,4,64]{2,1,0:T(4,128)S(1)}, s32[1,4,64]{2,1,0:T(4,128)}, u32[]{:S(2)}) copy-start(s32[1,4,64]{2,1,0:T(4,128)} %param.9) | copy-start | bytes 3076
  0.7 0.9 %copy-start.2 = (s32[1,64]{1,0:T(1,128)S(1)}, s32[1,64]{1,0:T(1,128)}, u32[]{:S(2)}) copy-start(s32[1,64]{1,0:T(1,128)} %lskel_s.1) | copy-start | bytes 772
  0.7 0.9 %copy-start.3 = (bf16[3,16]{1,0:T(4,128)(2,1)S(1)}, bf16[3,16]{1,0:T(4,128)(2,1)}, u32[]{:S(2)}) copy-start(bf16[3,16]{1,0:T(4,128)(2,1)} %panel_ref.1) | copy-start | bytes 292

commit v2 on v1

--- a/solution.py
+++ b/solution.py
@@ -28,12 +28,14 @@
 ROWS = LEAF + TREE
 HALF = LEAF // 2
 POOL = HALF + SK + TREE
-UNIT = 256
-GROUPS = ((0, 8),)
+UNIT = 512
+UNITS = 8
+EARLY = 4
+AHEAD = 4
 
 TURNS = KAPPA / (2.0 * math.pi)
 SIN_C = (4.442867902958649, -7.307443418384947, 3.5947880506885697, -0.7843739567847821)
-COS_C = (1.41421349656788, -6.97885098835421, 5.739461171797141, -1.8835629903414894, 0.3106981920345144)
+COS_C = (1.414204080778755, -6.977642063413481, 5.7152384214203416, -1.728348662706757)
 
 
 def horner(q, coefs):
@@ -92,33 +94,27 @@
 
 def pick_points(points, picks):
     n = points.shape[1]
-    hot = lax.broadcasted_iota(jnp.int32, (n, SK), 0) == picks
-    return jnp.dot(points, hot.astype(F32), precision=HI, preferred_element_type=F32)
-
-
-def group_rows(g):
-    return (GROUPS[g][1] + 1) * 16
-
-
-def group_base(g):
-    return sum(32 * group_rows(i) for i in range(g))
-
-
-def ring_dist(t, n):
-    return min(t % n, -t % n)
-
-
+    hot = (lax.broadcasted_iota(jnp.int32, (n, SK), 0) == picks).astype(BF16)
+    parts = jnp.concatenate(split3(points), axis=0).astype(BF16)
+    got = jnp.dot(parts, hot, preferred_element_type=F32)
+    return (got[0:8] + got[8:16]) + got[16:24]
+
+
+BLOCK = 144
 LINE = (4, 3, 5, 2, 6, 1, 7)
+
+
 PLANE = sorted(
-    [(i, k) for i in range(NX) for k in range(NZ) if (i, k) != (0, 0)],
-    key=lambda t: ring_dist(t[0], NX) + ring_dist(t[1], NZ),
+    [(i, k) for i in range(NX) for k in range(NZ)],
+    key=lambda t: min(t[0], NX - t[0]) + min(t[1], NZ - t[1]),
 )
 
 
 def sample_kernel(
-    pts_ref, panel_ref, vec_ref, lskel_ref, nskel_ref, lskel_s, out_ref,
-    raw, gath, tgt, u_s, k_re, k_im, acc, own_s, swap_tx, swap_rx, rx,
-    raw_send, raw_recv, g_send, g_recv, t_send, t_recv, x_send, x_recv,
+    pts_hbm, panel_ref, vec_hbm, lskel_hbm, nskel_hbm, out_ref,
+    pts_ref, lskel_ref, nskel_ref, lskel_s,
+    raw, gath, feat_s, vec_s, tgt, u_s, k_re, k_im, acc, own_s, swap_tx, swap_rx, rx,
+    raw_send, raw_recv, g_send, g_recv, t_send, t_recv, x_send, x_recv, in_sem,
 ):
     row = lax.axis_index("rows")
     col = lax.axis_index("cols")
@@ -129,39 +125,52 @@
     step_a = jnp.where(first, 1, 8)
     step_b = jnp.where(first, 8, 1)
 
-    def on_line(j):
-        return {"rows": row + ((a + j) % 8 - a) * step_a}
-
-    def on_plane(i, k):
-        return {"rows": row + ((x + i) % 4 - x) * 64 + ((b + k) % 8 - b) * step_b}
+    def wrapped(at, by, n):
+        return jnp.where(at + by >= n, at + by - n, at + by)
+
+    line = {j: {"rows": row + (wrapped(a, j, 8) - a) * step_a} for j in LINE}
+    hop_x = [(wrapped(x, i, NX) - x) * 64 for i in range(NX)]
+    hop_b = [(wrapped(b, k, NZ) - b) * step_b for k in range(NZ)]
+    plane = [{"rows": row + hop_x[i] + hop_b[k]} for i, k in PLANE]
 
     barrier = pltpu.get_barrier_semaphore()
-    peers = [on_line(j) for j in LINE] + [on_plane(*t) for t in PLANE] + [{"cols": 1 - col}]
+    peers = list(line.values()) + plane[1:] + [{"cols": 1 - col}]
     for peer in peers:
         pl.semaphore_signal(barrier, inc=1, device_id=peer, device_id_type=MESH)
+
+    mine = pl.ds(pl.multiple_of(a * 32, 32), 16)
+    loads = [
+        pltpu.make_async_copy(src, dst, in_sem.at[i])
+        for i, (src, dst) in enumerate(
+            ((vec_hbm, raw.at[mine]), (pts_hbm, pts_ref), (lskel_hbm, lskel_ref), (nskel_hbm, nskel_ref), (lskel_hbm, lskel_s))
+        )
+    ]
+    for load in loads:
+        load.start()
 
     eye = (
         lax.broadcasted_iota(jnp.int32, (16, 16), 0) == lax.broadcasted_iota(jnp.int32, (16, 16), 1)
     ).astype(BF16)
-    mine = pl.ds(pl.multiple_of(a * 32, 32), 16)
     mine_f = pl.ds(pl.multiple_of(a * 32 + 16, 16), 16)
     mine_both = pl.ds(pl.multiple_of(a * 32, 32), 32)
-    raw[mine] = lax.dot_general(eye, vec_ref[...], NT, preferred_element_type=F32).astype(BF16)
     feats = jnp.concatenate([source_features(panel_ref[...].astype(F32))] * 8, axis=0)
     slot = lax.broadcasted_iota(jnp.int32, (128, 16), 0) // 16
     feats = jnp.where(slot == a, feats, 0.0).astype(BF16)
     raw[mine_f] = lax.dot_general(eye, feats, NT, preferred_element_type=F32).astype(BF16)
 
+    loads[0].wait()
     pl.semaphore_wait(barrier, len(peers))
 
+    def raw_copy(j):
+        return pltpu.make_async_remote_copy(
+            raw.at[mine_both], raw.at[mine_both], raw_send, raw_recv.at[j], device_id=line[j], device_id_type=MESH
+        )
+
     for j in LINE:
-        pltpu.make_async_remote_copy(
-            raw.at[mine_both], raw.at[mine_both], raw_send, raw_recv.at[j], device_id=on_line(j), device_id_type=MESH
-        ).start()
-
-    zero_row = jnp.zeros((5, LEAF), F32)
-    points = jnp.concatenate([pts_ref[...], zero_row], axis=0)
-    current = pick_points(points, lskel_ref[...])
+        raw_copy(j).start()
+
+    for load in loads[1:]:
+        load.wait()
 
     def swap_copy(lev):
         bit = (row // (1 << lev)) % 2
@@ -184,85 +193,98 @@
         other = jnp.where(bit == 1, got[:, :SK], got[:, SK:])
         tgt[LEAF + lev * SK : LEAF + (lev + 1) * SK] = target_rows(other)
         both = swap_tx[lev] + got
-        return pick_points(both, nskel_ref[lev : lev + 1, :])
-
-    swap_start(0, current)
+        if lev + 1 < LEVELS:
+            swap_start(lev + 1, pick_points(both, nskel_ref[lev : lev + 1, :]))
+
+    zero_row = jnp.zeros((5, LEAF), F32)
+    points = jnp.concatenate([pts_ref[...], zero_row], axis=0)
+    swap_start(0, pick_points(points, lskel_ref[...]))
     tgt[0:LEAF] = target_rows(pts_ref[...])
     acc[...] = jnp.zeros_like(acc)
 
-    def block_copy(g, n, i, k):
-        rows = group_rows(g)
-        base = group_base(g)
+    lane = lax.broadcasted_iota(jnp.int32, (16, 128), 1) // 16
+
+    def block_copy(n, dev):
         return pltpu.make_async_remote_copy(
-            gath.at[pl.ds(base, rows)], gath.at[pl.ds(base + n * rows, rows)], g_send.at[g], g_recv.at[g, n],
-            device_id=on_plane(i, k), device_id_type=MESH,
+            gath.at[pl.ds(0, BLOCK)], gath.at[pl.ds(pl.multiple_of(n * BLOCK, 16), BLOCK)], g_send, g_recv.at[n],
+            device_id=dev, device_id_type=MESH,
         )
 
-    def send_group(g):
-        start, count = GROUPS[g]
-        base = group_base(g)
-        for j in range(1, 8):
-            src = (a + 8 - j) % 8
-            needed = jnp.logical_and(src >= start, src < start + count)
-
-            @pl.when(needed)
-            def _():
-                pltpu.make_async_remote_copy(
-                    raw.at[mine_both], raw.at[mine_both], raw_send, raw_recv.at[j], device_id=on_line(j), device_id_type=MESH
-                ).wait_recv()
-
-        feat = jnp.zeros((16, 128), BF16)
-        for i in range(count):
-            at = (start + i) * 32
-            gath[base + 16 * i : base + 16 * i + 16] = raw[at : at + 16]
-            feat = feat + raw[at + 16 : at + 32]
-        gath[base + 16 * count : base + 16 * count + 16] = feat
-        for n, (i, k) in enumerate(PLANE):
-            block_copy(g, n + 1, i, k).start()
-
-    lane = lax.broadcasted_iota(jnp.int32, (16, 128), 1) // 16
-
-    def compute_unit(g, unit):
-        start, count = GROUPS[g]
-        rows = group_rows(g)
-        srcs = UNIT // (16 * count)
-        vecs, feats = [], []
-        for s in range(srcs):
-            n = unit * srcs + s
+    swap_finish(0)
+    for j in LINE:
+        raw_copy(j).wait_recv()
+    feat = jnp.zeros((16, 128), BF16)
+    for i in range(8):
+        gath[16 * i : 16 * i + 16] = raw[32 * i : 32 * i + 16]
+        feat = feat + raw[32 * i + 16 : 32 * i + 32]
+    gath[128:144] = feat
+    per_unit = UNIT // 128
+
+    def send_unit(unit):
+        for n in range(max(1, unit * per_unit), (unit + 1) * per_unit):
+            block_copy(n, plane[n]).start()
+
+    for unit in range(AHEAD):
+        send_unit(unit)
+    swap_finish(1)
+
+    def fetch(unit):
+        for s in range(per_unit):
+            n = unit * per_unit + s
 
             @pl.when(n > 0)
-            def _():
-                block_copy(g, n, 0, 1).wait_recv()
-
-            at = group_base(g) + n * rows
-            vecs.append(gath[pl.ds(pl.multiple_of(at, 16), 16 * count)])
-            tile = gath[pl.ds(pl.multiple_of(at + 16 * count, 16), 16)]
-            for j in range(start, start + count):
-                feats.append(jnp.where(lane == j, tile, jnp.zeros_like(tile)))
-        feat = jnp.concatenate(feats, axis=0)
-        vec = jnp.concatenate(vecs, axis=0)
-        u_s[...] = lax.dot_general(tgt[...], feat, NT, preferred_element_type=F32)
-        for r in range(0, ROWS, 32):
-            re, im = kernel_values(u_s[r : r + 32])
-            k_re[r : r + 32] = re
-            k_im[r : r + 32] = im
-        acc[:, :VEC] += jnp.dot(k_re[...], vec, preferred_element_type=F32)
-        acc[:, VEC:] += jnp.dot(k_im[...], vec, preferred_element_type=F32)
-
-    for g in range(len(GROUPS)):
-        send_group(g)
-    for lev in range(LEVELS):
-        current = swap_finish(lev)
-        if lev + 1 < LEVELS:
-            swap_start(lev + 1, current)
-    for g in range(len(GROUPS)):
-        units = 32 * 16 * GROUPS[g][1] // UNIT
-
-        def step(u, carry, g=g):
-            compute_unit(g, u)
-            return carry
-
-        lax.fori_loop(0, units, step, 0)
+            def _(n=n):
+                block_copy(n, plane[1]).wait_recv()
+
+            at = pl.multiple_of(n * BLOCK, 16)
+            here = pl.multiple_of(unit * UNIT + s * 128, 128)
+            vec_s[pl.ds(here, 128)] = gath[pl.ds(at, 128)]
+            tile = gath[pl.ds(pl.multiple_of(at + 128, 16), 16)]
+            feat_s[pl.ds(here, 128)] = jnp.concatenate(
+                [jnp.where(lane == j, tile, jnp.zeros_like(tile)) for j in range(8)], axis=0
+            )
+
+    def add_unit(unit, lo, hi):
+        cols = pl.ds(pl.multiple_of(unit * UNIT, UNIT), UNIT)
+        vec = vec_s[cols]
+        u_s[lo:hi] = lax.dot_general(tgt[lo:hi], feat_s[cols], NT, preferred_element_type=F32)
+        for r in range(lo, hi, 16):
+            re, im = kernel_values(u_s[r : r + 16])
+            k_re[r : r + 16] = re
+            k_im[r : r + 16] = im
+        acc[lo:hi, :VEC] += jnp.dot(k_re[lo:hi], vec, preferred_element_type=F32)
+        acc[lo:hi, VEC:] += jnp.dot(k_im[lo:hi], vec, preferred_element_type=F32)
+
+    def leaf_unit(unit, carry):
+        for u in range(EARLY):
+            if u + AHEAD < UNITS:
+                @pl.when(unit == u)
+                def _(u=u):
+                    send_unit(u + AHEAD)
+        fetch(unit)
+        add_unit(unit, 0, LEAF)
+        for lev, after in ((2, 0), (3, EARLY - 1)):
+            @pl.when(unit == after)
+            def _(lev=lev):
+                swap_finish(lev)
+        return carry
+
+    def tree_unit(unit, carry):
+        for u in range(EARLY + AHEAD, UNITS):
+            @pl.when(unit == u - EARLY - AHEAD)
+            def _(u=u):
+                send_unit(u)
+        add_unit(unit, LEAF, ROWS)
+        return carry
+
+    def full_unit(unit, carry):
+        fetch(unit)
+        add_unit(unit, 0, ROWS)
+        return carry
+
+    lax.fori_loop(0, EARLY, leaf_unit, 0)
+    lax.fori_loop(0, EARLY, tree_unit, 0)
+    lax.fori_loop(EARLY, UNITS, full_unit, 0)
 
     for k in range(SK):
         own_s[k : k + 1] = acc[pl.ds(lskel_s[0, k], 1)]
@@ -292,27 +314,29 @@
     for lev in range(LEVELS):
         swap_copy(lev).wait_send()
     for j in LINE:
-        pltpu.make_async_remote_copy(
-            raw.at[mine_both], raw.at[mine_both], raw_send, raw_recv.at[j], device_id=on_line(j), device_id_type=MESH
-        ).wait_send()
-    for g in range(len(GROUPS)):
-        for n, (i, k) in enumerate(PLANE):
-            block_copy(g, n + 1, i, k).wait_send()
+        raw_copy(j).wait_send()
+    for n in range(1, 32):
+        block_copy(n, plane[n]).wait_send()
 
 
 def sample_rows(row_points, panel_points, test_vectors, leaf_skeleton, node_skeleton):
     vmem = pl.BlockSpec(memory_space=pltpu.VMEM)
-    n_groups = len(GROUPS)
-    gath_rows = group_base(n_groups)
+    hbm = pl.BlockSpec(memory_space=pltpu.HBM)
     dma = pltpu.SemaphoreType.DMA
     return pl.pallas_call(
         sample_kernel,
         out_shape=jax.ShapeDtypeStruct((POOL, 2 * VEC), F32),
-        in_specs=[vmem] * 5 + [pl.BlockSpec(memory_space=pltpu.SMEM)],
+        in_specs=[hbm, vmem, hbm, hbm, hbm],
         out_specs=vmem,
         scratch_shapes=[
+            pltpu.VMEM(row_points.shape, F32),
+            pltpu.VMEM((1, SK), jnp.int32),
+            pltpu.VMEM((LEVELS, SK), jnp.int32),
+            pltpu.SMEM((1, SK), jnp.int32),
             pltpu.VMEM((256, 128), BF16),
-            pltpu.VMEM((gath_rows, 128), BF16),
+            pltpu.VMEM((32 * BLOCK, 128), BF16),
+            pltpu.VMEM((UNITS * UNIT, 128), BF16),
+            pltpu.VMEM((UNITS * UNIT, 128), BF16),
             pltpu.VMEM((ROWS, 128), BF16),
             pltpu.VMEM((ROWS, UNIT), F32),
             pltpu.VMEM((ROWS, UNIT), BF16),
@@ -324,16 +348,17 @@
             pltpu.VMEM((POOL, 2 * VEC), F32),
             dma,
             dma((8,)),
-            dma((n_groups,)),
-            dma((n_groups, 32)),
+            dma,
+            dma((32,)),
             dma((LEVELS,)),
             dma((LEVELS,)),
             dma((3,)),
             dma((3,)),
+            dma((5,)),
         ],
         compiler_params=pltpu.CompilerParams(collective_id=1, has_side_effects=True, vmem_limit_bytes=40 << 20),
         name="sample_rows",
-    )(row_points, panel_points, test_vectors, leaf_skeleton, node_skeleton[0], leaf_skeleton)
+    )(row_points, panel_points, test_vectors.T, leaf_skeleton, node_skeleton[0])
 
 
 SPREAD = 1.0 + SK / RIDGE

time: 64.5 us -> 53.3 us (0.83)
  Pallas kernels: 62.4 us -> 50.3 us
  local copies, waits for them, and re-layouts: 0.84 us -> 2.06 us
    pallas_call x1, Pallas kernels: 57.7 us -> 45.6 us  [sample_rows(): pl.pallas_call(sample_kernel, out_shape=jax.ShapeDtypeStruct((POOL, 2 * V...]
    unnamed x9 -> x10, local copies, waits for them, and re-layouts: 0.84 us -> 2.06 us
where the time goes in v2:
time: 53.3 us; the launch traced here: 53.1 us
  Pallas kernels  50.3 us (94%)
  local copies, waits for them, and re-layouts  2.06 us (4%)
  between operations  0.67 us (1%)
    pallas_call x1, Pallas kernels, sample_rows(): pl.pallas_call(sample_kernel, out_shape=jax.ShapeDtypeStruct((POOL, 2 * V...  45.6 us
    pallas_call x1, Pallas kernels, solve(): pl.pallas_call(solve_kernel, out_shape=(jax.ShapeDtypeStruct((SK, HALF),...  4.73 us
    unnamed x10, local copies, waits for them, and re-layouts  2.06 us

profile of v2, /device:TPU:1, one launch (start us, length us, event | category | flops | bytes accessed | tf_op | source)
XLA Modules:
  0.0 53.1 jit_solution(2504996716834502657)
XLA Ops:
  0.6 0.0 copy-start.1
  0.6 0.0 copy-start.3
  0.7 0.0 copy-start.4
  0.7 0.7 %copy-done.1 = s32[1,4,64]{2,1,0:T(4,128)S(1)} copy-done((s32[1,4,64]{2,1,0:T(4,128)S(1)}, s32[1,4,64]{2,1,0:T(4,128)}, u32[]{:S(2)}) %copy-start.1) | copy-done | bytes 1048
  1.3 0.0 copy-done.3
  1.3 0.0 copy-done.4
  1.3 0.0 copy-start
  1.3 0.7 %copy-done = f32[3,512]{1,0:T(4,128)S(1)} copy-done((f32[3,512]{1,0:T(4,128)S(1)}, f32[3,512]{1,0:T(4,128)}, u32[]{:S(2)}) %copy-start) | copy-done | bytes 6168
  2.0 0.0 copy-start.2
  2.0 0.7 %copy-done.2 = bf16[128,16]{0,1:T(8,128)(2,1)S(1)} copy-done((bf16[128,16]{0,1:T(8,128)(2,1)S(1)}, bf16[128,16]{0,1:T(8,128)(2,1)}, u32[]{:S(2)}) %copy-start.2) | copy-done | bytes 4120
  2.7 45.6 %sample_rows.1.pool_ref = f32[576,256]{1,0:T(8,128)S(1)} custom-call(f32[3,512]{1,0:T(4,128)S(1)} %copy-done, bf16[3,16]{1,0:T(4,128)(2,1)S(1)} %copy-done.3, bf16[16,128]{1,0:T(8,128)(2,1)S(1)} %bitcast.4, s32[1,64]{1,0:T(1,128)S(1)} %copy-done.4, s32[4,64]{1,0:T(4,128)S(1)} %bitcast.2), custom_call_target="tpu_custom_call" | custom-call | tf_op jit(solution)/shard_map/sample_rows/pallas_call | solution.py:326
  48.3 4.7 %solve.1 = (f32[64,256]{1,0:T(8,128)}, f32[1,4,64,128]{3,2,1,0:T(8,128)}, f32[1,64,256]{2,1,0:T(8,128)}) custom-call(f32[576,256]{1,0:T(8,128)S(1)} %sample_rows.1.pool_ref, s32[4,64]{1,0:T(4,128)S(1)} %bitcast.3), custom_call_target="tpu_custom_call" | custom-call | tf_op jit(solution)/shard_map/solve/pallas_call | solution.py:420
Async XLA Ops:
  0.6 0.7 %copy-start.1 = (s32[1,4,64]{2,1,0:T(4,128)S(1)}, s32[1,4,64]{2,1,0:T(4,128)}, u32[]{:S(2)}) copy-start(s32[1,4,64]{2,1,0:T(4,128)} %param.9) | copy-start | bytes 3076
  0.6 0.7 %copy-start.3 = (bf16[3,16]{1,0:T(4,128)(2,1)S(1)}, bf16[3,16]{1,0:T(4,128)(2,1)}, u32[]{:S(2)}) copy-start(bf16[3,16]{1,0:T(4,128)(2,1)} %panel_ref.1) | copy-start | bytes 292
  0.7 0.7 %copy-start.4 = (s32[1,64]{1,0:T(1,128)S(1)}, s32[1,64]{1,0:T(1,128)}, u32[]{:S(2)}) copy-start(s32[1,64]{1,0:T(1,128)} %lskel_hbm.1) | copy-start | bytes 772
  1.3 0.7 %copy-start = (f32[3,512]{1,0:T(4,128)S(1)}, f32[3,512]{1,0:T(4,128)}, u32[]{:S(2)}) copy-start(f32[3,512]{1,0:T(4,128)} %pts_hbm.1) | copy-start | bytes 18436
  2.0 0.7 %copy-start.2 = (bf16[128,16]{0,1:T(8,128)(2,1)S(1)}, bf16[128,16]{0,1:T(8,128)(2,1)}, u32[]{:S(2)}) copy-start(bf16[128,16]{0,1:T(8,128)(2,1)} %param.7) | copy-start | bytes 12292

commit v3 on v2

--- a/solution.py
+++ b/solution.py
@@ -111,7 +111,7 @@
 
 
 def sample_kernel(
-    pts_hbm, panel_ref, vec_hbm, lskel_hbm, nskel_hbm, out_ref,
+    pts_hbm, panel_ref, vec_ref, lskel_hbm, nskel_hbm, out_ref,
     pts_ref, lskel_ref, nskel_ref, lskel_s,
     raw, gath, feat_s, vec_s, tgt, u_s, k_re, k_im, acc, own_s, swap_tx, swap_rx, rx,
     raw_send, raw_recv, g_send, g_recv, t_send, t_recv, x_send, x_recv, in_sem,
@@ -142,7 +142,7 @@
     loads = [
         pltpu.make_async_copy(src, dst, in_sem.at[i])
         for i, (src, dst) in enumerate(
-            ((vec_hbm, raw.at[mine]), (pts_hbm, pts_ref), (lskel_hbm, lskel_ref), (nskel_hbm, nskel_ref), (lskel_hbm, lskel_s))
+            ((pts_hbm, pts_ref), (lskel_hbm, lskel_ref), (nskel_hbm, nskel_ref), (lskel_hbm, lskel_s))
         )
     ]
     for load in loads:
@@ -156,9 +156,9 @@
     feats = jnp.concatenate([source_features(panel_ref[...].astype(F32))] * 8, axis=0)
     slot = lax.broadcasted_iota(jnp.int32, (128, 16), 0) // 16
     feats = jnp.where(slot == a, feats, 0.0).astype(BF16)
+    raw[mine] = lax.dot_general(eye, vec_ref[...], NT, preferred_element_type=F32).astype(BF16)
     raw[mine_f] = lax.dot_general(eye, feats, NT, preferred_element_type=F32).astype(BF16)
 
-    loads[0].wait()
     pl.semaphore_wait(barrier, len(peers))
 
     def raw_copy(j):
@@ -169,7 +169,7 @@
     for j in LINE:
         raw_copy(j).start()
 
-    for load in loads[1:]:
+    for load in loads:
         load.wait()
 
     def swap_copy(lev):
@@ -326,7 +326,7 @@
     return pl.pallas_call(
         sample_kernel,
         out_shape=jax.ShapeDtypeStruct((POOL, 2 * VEC), F32),
-        in_specs=[hbm, vmem, hbm, hbm, hbm],
+        in_specs=[hbm, vmem, vmem, hbm, hbm],
         out_specs=vmem,
         scratch_shapes=[
             pltpu.VMEM(row_points.shape, F32),
@@ -354,11 +354,11 @@
             dma((LEVELS,)),
             dma((3,)),
             dma((3,)),
-            dma((5,)),
+            dma((4,)),
         ],
         compiler_params=pltpu.CompilerParams(collective_id=1, has_side_effects=True, vmem_limit_bytes=40 << 20),
         name="sample_rows",
-    )(row_points, panel_points, test_vectors.T, leaf_skeleton, node_skeleton[0])
+    )(row_points, panel_points, test_vectors, leaf_skeleton, node_skeleton[0])
 
 
 SPREAD = 1.0 + SK / RIDGE
@@ -386,6 +386,15 @@
 
     def mm(p, q):
         return jnp.dot(p, q, precision=HI, preferred_element_type=F32)
+
+    def halves(p):
+        hi = p.astype(BF16)
+        return hi, (p - hi.astype(F32)).astype(BF16)
+
+    def mm3(p, q):
+        (ph, pl_), (qh, ql) = p, q
+        dot = functools.partial(jnp.dot, preferred_element_type=F32)
+        return dot(ph, qh) + (dot(ph, ql) + dot(pl_, qh))
 
     work = []
     for skel, block in systems:
@@ -404,12 +413,14 @@
         next_inv, next_prod = [], []
         for inv, prod in zip(inverses, prods):
             left = (2.0 * eye - prod) * factor
-            next_inv.append(left if it == 0 else mm(left, inv))
-            next_prod.append(mm(left, prod) if it + 1 < NEWTON else prod)
+            parts = halves(left)
+            next_inv.append(left if it == 0 else mm3(parts, halves(inv)))
+            next_prod.append(mm3(parts, halves(prod)) if it + 1 < NEWTON else prod)
         inverses, prods = next_inv, next_prod
-    sols = [mm(inv, right) for inv, (_, right) in zip(inverses, work)]
+    inverses = [halves(inv) for inv in inverses]
+    sols = [mm3(inv, halves(right)) for inv, (_, right) in zip(inverses, work)]
     rest = [right - mm(m, sol) for sol, (m, right) in zip(sols, work)]
-    sols = [sol + mm(inv, r) for sol, inv, r in zip(sols, inverses, rest)]
+    sols = [sol + mm3(inv, halves(r)) for sol, inv, r in zip(sols, inverses, rest)]
     interp_ref[...] = sols[0]
     for lev in range(LEVELS):
         maps_ref[0, lev] = sols[lev + 1]

time: 53.3 us -> 51.4 us (0.964)
  local copies, waits for them, and re-layouts: 2.06 us -> 0.84 us
  Pallas kernels: 50.3 us -> 49.7 us
    unnamed x10 -> x9, local copies, waits for them, and re-layouts: 2.06 us -> 0.84 us
    pallas_call x1, Pallas kernels: 4.73 us -> 4.1 us  [solve(): pl.pallas_call(solve_kernel, out_shape=(jax.ShapeDtypeStruct((SK, HALF),...]
where the time goes in v3:
time: 51.4 us; the launch traced here: 51.2 us
  Pallas kernels  49.7 us (97%)
  local copies, waits for them, and re-layouts  0.84 us (2%)
  between operations  0.7 us (1%)
    pallas_call x1, Pallas kernels, sample_rows(): pl.pallas_call(sample_kernel, out_shape=jax.ShapeDtypeStruct((POOL, 2 * V...  45.6 us
    pallas_call x1, Pallas kernels, solve(): pl.pallas_call(solve_kernel, out_shape=(jax.ShapeDtypeStruct((SK, HALF),...  4.1 us

profile of v3, /device:TPU:1, one launch (start us, length us, event | category | flops | bytes accessed | tf_op | source)
XLA Modules:
  0.0 51.2 jit_solution(14858023569058079516)
XLA Ops:
  0.6 0.0 copy-start
  0.6 0.0 copy-start.1
  0.7 0.0 copy-start.2
  0.7 0.0 copy-start.3
  0.7 0.8 %copy.8.vec_ref = bf16[128,16]{1,0:T(8,128)(2,1)S(1)} copy(bf16[128,16]{0,1:T(8,128)(2,1)} %param.7) | data formatting | bytes 8192 | tf_op args[2]
  1.5 0.0 copy-done
  1.5 0.0 copy-done.1
  1.5 0.0 copy-done.2
  1.5 0.0 copy-done.3
  1.5 45.6 %sample_rows.1.pool_ref = f32[576,256]{1,0:T(8,128)S(1)} custom-call(f32[3,512]{1,0:T(4,128)S(1)} %copy-done, bf16[3,16]{1,0:T(4,128)(2,1)S(1)} %copy-done.2, bf16[128,16]{1,0:T(8,128)(2,1)S(1)} %copy.8.vec_ref, s32[1,64]{1,0:T(1,128)S(1)} %copy-done.3, s32[4,64]{1,0:T(4,128)S(1)} %bitcast.1), custom_call_target="tpu_custom_call" | custom-call | tf_op jit(solution)/shard_map/sample_rows/pallas_call | solution.py:326
  47.1 4.1 %solve.1 = (f32[64,256]{1,0:T(8,128)}, f32[1,4,64,128]{3,2,1,0:T(8,128)}, f32[1,64,256]{2,1,0:T(8,128)}) custom-call(f32[576,256]{1,0:T(8,128)S(1)} %sample_rows.1.pool_ref, s32[4,64]{1,0:T(4,128)S(1)} %bitcast.2), custom_call_target="tpu_custom_call" | custom-call | tf_op jit(solution)/shard_map/solve/pallas_call | solution.py:431
Async XLA Ops:
  0.6 0.9 %copy-start = (f32[3,512]{1,0:T(4,128)S(1)}, f32[3,512]{1,0:T(4,128)}, u32[]{:S(2)}) copy-start(f32[3,512]{1,0:T(4,128)} %pts_hbm.1) | copy-start | bytes 18436
  0.6 0.9 %copy-start.1 = (s32[1,4,64]{2,1,0:T(4,128)S(1)}, s32[1,4,64]{2,1,0:T(4,128)}, u32[]{:S(2)}) copy-start(s32[1,4,64]{2,1,0:T(4,128)} %param.9) | copy-start | bytes 3076
  0.7 0.9 %copy-start.2 = (bf16[3,16]{1,0:T(4,128)(2,1)S(1)}, bf16[3,16]{1,0:T(4,128)(2,1)}, u32[]{:S(2)}) copy-start(bf16[3,16]{1,0:T(4,128)(2,1)} %panel_ref.1) | copy-start | bytes 292
  0.7 0.9 %copy-start.3 = (s32[1,64]{1,0:T(1,128)S(1)}, s32[1,64]{1,0:T(1,128)}, u32[]{:S(2)}) copy-start(s32[1,64]{1,0:T(1,128)} %lskel_hbm.1) | copy-start | bytes 772
